TPU v7x, 128 devices: a whole 4x4x4 slice. The times are simulated.
128 devices in a mesh: seq: 32 (over y, z, core), head: 4 (over x).
Axes of the slice: x: 4, y: 4, z: 4, core: 2. Of those that a mesh axis runs over, the one named last changes fastest.
Arguments:
- query_rows: bfloat16 [32768, 5120], P(('seq', 'head')), may hold values from -6 to 6
- key_rows: bfloat16 [32768, 5120], P(('seq', 'head')), may hold values from -6 to 6
- value_rows: bfloat16 [32768, 5120], P(('seq', 'head')), may hold values from -6 to 6
- log_decay: bfloat16 [32768, 40], P(('seq', 'head')), may hold values from -1 to 0
- documents: int32 [32768], replicated, may hold values from 0 to 2, as said below
- norm_gain: float32 [5120], replicated, may hold values from 0.25 to 1.75
Outputs:
- attended: bfloat16 [32768, 5120], P(('seq', 'head'))
Inputs may be any that keep to these rules, and one draw needn't show every extreme that they name: `documents`: document numbers never fall along the tokens and each of the 3 numbers occurs.
All inputs are finite; a program needn't handle non-finite values.
Results may differ from a plain program's by a relative error of at most 0.0056.
Values may be sent and summed in bfloat16 or wider, within the bound.
No kernel may reach another device: no remote copies, remote signals or barrier semaphores. Data moves between devices by JAX's collectives and lax.ppermute only.
A program may use at most 640 MiB of HBM per device.

v0:
```python
import jax
import jax.numpy as jnp
from jax import lax
from jax.sharding import PartitionSpec as P

BLOCK = 256


def prefix(part, axis, combine, identity):
    place = lax.axis_index(axis)
    gathered = jax.tree.map(lambda a: lax.all_gather(a, axis), part)
    state = jax.tree.map(lambda a, e: jnp.zeros_like(a) + jnp.asarray(e, a.dtype), part, identity)

    def one(lap, state):
        return combine(
            state, jax.tree.map(lambda a: lax.dynamic_index_in_dim(a, lap, 0, False), gathered)
        )

    return lax.fori_loop(0, place, one, state)


def combine_states(earlier, later):
    return (earlier[0] * later[0], later[0][:, None, None] * earlier[1] + later[1])


def block_local(query_blocks, key_blocks, value_blocks, cumulative, doc_blocks):
    span = query_blocks.shape[1]
    scores = jnp.einsum(
        "nchd,nshd->nhcs", query_blocks, key_blocks, preferred_element_type=jnp.float32
    )
    cum_heads = jnp.swapaxes(cumulative, 1, 2)
    exponent = cum_heads[:, :, :, None] - cum_heads[:, :, None, :]
    causal = jnp.arange(span)[:, None] >= jnp.arange(span)[None, :]
    allowed = (causal[None] & (doc_blocks[:, :, None] == doc_blocks[:, None, :]))[:, None]
    decay_mask = jnp.where(allowed, jnp.exp(jnp.where(allowed, exponent, 0.0)), 0.0)
    weights = (scores * decay_mask).astype(jnp.bfloat16)
    return jnp.einsum("nhcs,nshd->nchd", weights, value_blocks, preferred_element_type=jnp.float32)


def attend(query, keyed, valued, decays, documents, first_row, gain_group, prefix_fn):
    row_count = query.shape[0]
    head_count = decays.shape[1]
    head_width = query.shape[1] // head_count
    block_count = row_count // BLOCK
    query_blocks = query.reshape(block_count, BLOCK, head_count, head_width)
    key_blocks = keyed.reshape(block_count, BLOCK, head_count, head_width)
    value_blocks = valued.reshape(block_count, BLOCK, head_count, head_width)
    cumulative = jnp.cumsum(
        decays.astype(jnp.float32).reshape(block_count, BLOCK, head_count), axis=1
    )
    local_docs = lax.dynamic_slice_in_dim(documents, first_row, row_count)
    doc_before = lax.dynamic_slice_in_dim(documents, jnp.maximum(first_row - 1, 0), 1)
    doc_blocks = local_docs.reshape(block_count, BLOCK)
    previous = jnp.concatenate([doc_before, doc_blocks[:-1, -1]])
    usable = (doc_blocks == previous[:, None]).astype(jnp.float32)
    final_cum = cumulative[:, -1, :]
    factor = jnp.exp(final_cum) * (doc_blocks[:, -1] == previous).astype(jnp.float32)[:, None]
    same_last = (doc_blocks == doc_blocks[:, -1:]).astype(jnp.float32)
    key_scale = jnp.exp(final_cum[:, None, :] - cumulative) * same_last[:, :, None]
    key_decayed = (key_blocks.astype(jnp.float32) * key_scale[..., None]).astype(jnp.bfloat16)
    block_state = jnp.einsum(
        "nchd,nche->nhde", key_decayed, value_blocks, preferred_element_type=jnp.float32
    )
    query_decayed = (
        query_blocks.astype(jnp.float32) * (jnp.exp(cumulative) * usable[:, :, None])[..., None]
    ).astype(jnp.bfloat16)

    def local_advance(carry, item):
        decay_so_far, state_so_far = carry
        block_factor, block_update = item
        return (
            (
                decay_so_far * block_factor,
                block_factor[:, None, None] * state_so_far + block_update,
            ),
            (decay_so_far, state_so_far),
        )

    start_carry = (
        jnp.ones((head_count,), jnp.float32),
        jnp.zeros((head_count, head_width, head_width), jnp.float32),
    )
    summary, entering = lax.scan(local_advance, start_carry, (factor, block_state))
    incoming = prefix_fn(summary)[1]

    def advance(carried_state, item):
        query_one, key_one, value_one, cum_one, doc_one, decayed_one, factor_one, update_one = item
        within = block_local(
            query_one[None], key_one[None], value_one[None], cum_one[None], doc_one[None]
        )[0]
        carried = jnp.einsum(
            "chd,hde->che",
            decayed_one,
            carried_state.astype(jnp.bfloat16),
            preferred_element_type=jnp.float32,
        )
        return (factor_one[:, None, None] * carried_state + update_one, within + carried)

    _, outputs = lax.scan(
        advance,
        incoming,
        (
            query_blocks,
            key_blocks,
            value_blocks,
            cumulative,
            doc_blocks,
            query_decayed,
            factor,
            block_state,
        ),
    )
    mean_square = jnp.mean(outputs * outputs, axis=-1, keepdims=True)
    normed = outputs * lax.rsqrt(mean_square + 1e-05) * gain_group.reshape(head_count, head_width)
    return normed.astype(jnp.bfloat16).reshape(row_count, head_count * head_width)


def body(query_rows, key_rows, value_rows, log_decay, documents, norm_gain):
    query, keyed, valued, decays = (
        lax.all_to_all(query_rows, "head", split_axis=1, concat_axis=0, tiled=True),
        lax.all_to_all(key_rows, "head", split_axis=1, concat_axis=0, tiled=True),
        lax.all_to_all(value_rows, "head", split_axis=1, concat_axis=0, tiled=True),
        lax.all_to_all(log_decay, "head", split_axis=1, concat_axis=0, tiled=True),
    )
    row_count = query.shape[0]
    group_width = query.shape[1]
    first_row = lax.axis_index("seq") * row_count
    gain_group = lax.dynamic_slice_in_dim(
        norm_gain, lax.axis_index("head") * group_width, group_width
    )

    def prefix_group(summary):
        identity = (jnp.ones_like(summary[0]), jnp.zeros_like(summary[1]))
        return prefix((summary[0], summary[1]), "seq", combine_states, identity)

    grouped = attend(query, keyed, valued, decays, documents, first_row, gain_group, prefix_group)
    return lax.all_to_all(grouped, "head", split_axis=0, concat_axis=1, tiled=True)


def solution(mesh):
    placed = (
        P(("seq", "head"), None),
        P(("seq", "head"), None),
        P(("seq", "head"), None),
        P(("seq", "head"), None),
        P(),
        P(),
    )
    return jax.shard_map(
        body, mesh=mesh, in_specs=placed, out_specs=P(("seq", "head"), None), check_vma=False
    )
```

profile of v0, /device:TPU:121, one launch (start us, length us, event | category | flops | bytes accessed | tf_op | source)
XLA Modules:
  0.0 299.5 jit_solution(4036128251627386428)
XLA Ops:
  7.9 4.0 %all-to-all-start = ((bf16[256,4,10]{0,2,1:T(8,128)(2,1)}), bf16[256,4,10]{0,2,1:T(8,128)(2,1)S(1)}, u32[]{:S(2)}, u32[]{:S(2)}) async-start(bf16[256,4,10]{0,2,1:T(8,128)(2,1)} %all_to_all.60), calls=%async_computation | async-start | bytes 65536 | tf_op jit(solution)/shard_map/all_to_all | solution.py:123
  11.9 4.4 %copy.88 = bf16[256,5120]{0,1:T(8,128)(2,1)} copy(bf16[256,5120]{1,0:T(8,128)(2,1)} %param.13) | data formatting | bytes 5242880 | tf_op args[1]
  16.3 4.2 %all-to-all-start.1 = ((bf16[256,4,1280]{0,2,1:T(8,128)(2,1)}), bf16[256,4,1280]{0,2,1:T(8,128)(2,1)S(1)}, u32[]{:S(2)}, u32[]{:S(2)}) async-start(bf16[256,4,1280]{0,2,1:T(8,128)(2,1)} %bitcast.125), calls=%async_computation.1 | async-start | bytes 5242880 | tf_op jit(solution)/shard_map/all_to_all | solution.py:121
  20.5 4.4 %copy.91 = bf16[256,5120]{0,1:T(8,128)(2,1)} copy(bf16[256,5120]{1,0:T(8,128)(2,1)} %param.14) | data formatting | bytes 5242880 | tf_op args[2]
  24.9 26.1 %all-to-all-done.1 = bf16[256,4,1280]{0,2,1:T(8,128)(2,1)S(1)} async-done(((bf16[256,4,1280]{0,2,1:T(8,128)(2,1)}), bf16[256,4,1280]{0,2,1:T(8,128)(2,1)S(1)}, u32[]{:S(2)}, u32[]{:S(2)}) %all-to-all-start.1) | async-done | bytes 2621472 | tf_op jit(solution)/shard_map/all_to_all | solution.py:121
  52.5 4.6 %all-to-all-start.2 = ((bf16[256,4,1280]{0,2,1:T(8,128)(2,1)}), bf16[256,4,1280]{0,2,1:T(8,128)(2,1)}, u32[]{:S(2)}, u32[]{:S(2)}) async-start(bf16[256,4,1280]{0,2,1:T(8,128)(2,1)} %bitcast.123), calls=%async_computation.2 | async-start | bytes 5242880 | tf_op jit(solution)/shard_map/all_to_all | solution.py:122
  61.4 2.3 reduce-window.6
  64.5 22.2 %all-to-all-done.2 = bf16[256,4,1280]{0,2,1:T(8,128)(2,1)} async-done(((bf16[256,4,1280]{0,2,1:T(8,128)(2,1)}), bf16[256,4,1280]{0,2,1:T(8,128)(2,1)}, u32[]{:S(2)}, u32[]{:S(2)}) %all-to-all-start.2) | async-done | bytes 2621472 | tf_op jit(solution)/shard_map/all_to_all | solution.py:122
  86.7 3.4 %fusion.27 = f32[4,10,128,128]{3,2,1,0:T(8,128)S(1)} fusion(bf16[4,256,10,128]{1,3,2,0:T(8,128)(2,1)} %bitcast.27, bf16[4,256,10,128]{1,3,2,0:T(8,128)(2,1)} %bitcast.119, f32[4,256,10]{1,2,0:T(8,128)S(1)} %copy.90), kind=kOutput, calls=%fused_computation.41 | convolution fusion | flops 339476480 | bytes 7905280 | tf_op jit(solution)/shard_map/nchd,nche->nhde/dot_general | solution.py:61
  91.7 4.6 %copy.93 = bf16[256,5120]{0,1:T(8,128)(2,1)} copy(bf16[256,5120]{1,0:T(8,128)(2,1)} %param.12) | data formatting | bytes 5242880 | tf_op args[0]
  96.3 3.8 %all-to-all-start.3 = ((bf16[256,4,1280]{0,2,1:T(8,128)(2,1)}), bf16[256,4,1280]{0,2,1:T(8,128)(2,1)S(1)}, u32[]{:S(2)}, u32[]{:S(2)}) async-start(bf16[256,4,1280]{0,2,1:T(8,128)(2,1)} %bitcast.124), calls=%async_computation.3 | async-start | bytes 5242880 | tf_op jit(solution)/shard_map/all_to_all | solution.py:120
  101.9 63.2 %all-reduce = f32[320]{0:T(512)S(1)} all-reduce(f32[320]{0:T(512)S(1)} %dynamic-update-slice), channel_id=2, replica_groups=mesh['seq'=32,'head'=4] {'seq'}, use_global_device_ids=true, to_apply=%add | all-reduce | flops 320 | bytes 2560
  167.5 7.4 %all-gather.4.cloned.1.call-done = f32[320,128,128]{2,1,0:T(8,128)} async-done(((f32[10,128,128]{2,1,0:T(8,128)}), f32[320,128,128]{2,1,0:T(8,128)}) %all-gather.4.cloned.1.call-update) | async-done | bytes 20971536 | tf_op jit(solution)/shard_map/all_gather | solution.py:11
  174.9 40.4 %while.37 = (s32[]{:T(128)}, f32[10,128,128]{2,1,0:T(8,128)S(1)}, s32[]{:T(128)}, f32[32,10]{1,0:T(8,128)S(1)}, f32[32,10,128,128]{3,2,1,0:T(8,128)}, /*index=5*/s32[]{:T(128)}, s32[]{:T(128)}, s32[]{:T(128)}) while((s32[]{:T(128)}, f32[10,128,128]{2,1,0:T(8,128)S(1)}, s32[]{:T(128)}, f32[32,10]{1,0:T(8,128)S(1)}, ...), condition=%wide.region_5.6_spmd, body=%wide.region_4.5_spmd.sunk | while | flops 327685 | bytes 1966327 | solution.py:19
  215.4 27.1 %while.38 = (s32[]{:T(128)}, f32[10,128,128]{2,1,0:T(8,128)S(1)}, f32[4,256,10,128]{1,3,2,0:T(8,128)}, f32[4,10]{1,0:T(4,128)S(1)}, f32[4,10,128,128]{3,2,1,0:T(...) while((s32[]{:T(128)}, f32[10,128,128]{2,1,0:T(8,128)S(1)}, ...), condition=%wide.region_7.8_spmd, body=%wide.region_6.7_spmd.sunk | while | flops 423723008 | bytes 9385725 | solution.py:99
  217.0 3.8 %fusion.48 = f32[4,256,10,128]{1,3,2,0:T(8,128)} fusion(f32[4,256,10,128]{1,3,2,0:T(8,128)} %get-tuple-element.454, s32[]{:T(128)} %get-tuple-element.452, f32[256,10,128]{0,2,1:T(8,128)S(1)} %convolution_bitcast_fusion.3, f32[10,256]{1,0:T(8,128)S(1)} %bitcast.130, pred[256,256]{1,0:T(8,128)(4,1)S(1)} %fusion.47, ...), kind=kOutput, calls=%fused_computation.6.clone.1 | convolution fusion | flops 339148800 | bytes 4687872 | tf_op jit(solution)/shard_map/while/body/eval_jaxpr/nhcs,nshd->nchd/dot_general | solution.py:37
  223.8 3.9 %fusion.48 = f32[4,256,10,128]{1,3,2,0:T(8,128)} fusion(f32[4,256,10,128]{1,3,2,0:T(8,128)} %get-tuple-element.454, s32[]{:T(128)} %get-tuple-element.452, f32[256,10,128]{0,2,1:T(8,128)S(1)} %convolution_bitcast_fusion.3, f32[10,256]{1,0:T(8,128)S(1)} %bitcast.130, pred[256,256]{1,0:T(8,128)(4,1)S(1)} %fusion.47, ...), kind=kOutput, calls=%fused_computation.6.clone.1 | convolution fusion | flops 339148800 | bytes 4687872 | tf_op jit(solution)/shard_map/while/body/eval_jaxpr/nhcs,nshd->nchd/dot_general | solution.py:37
  230.6 3.8 %fusion.48 = f32[4,256,10,128]{1,3,2,0:T(8,128)} fusion(f32[4,256,10,128]{1,3,2,0:T(8,128)} %get-tuple-element.454, s32[]{:T(128)} %get-tuple-element.452, f32[256,10,128]{0,2,1:T(8,128)S(1)} %convolution_bitcast_fusion.3, f32[10,256]{1,0:T(8,128)S(1)} %bitcast.130, pred[256,256]{1,0:T(8,128)(4,1)S(1)} %fusion.47, ...), kind=kOutput, calls=%fused_computation.6.clone.1 | convolution fusion | flops 339148800 | bytes 4687872 | tf_op jit(solution)/shard_map/while/body/eval_jaxpr/nhcs,nshd->nchd/dot_general | solution.py:37
  237.3 3.9 %fusion.48 = f32[4,256,10,128]{1,3,2,0:T(8,128)} fusion(f32[4,256,10,128]{1,3,2,0:T(8,128)} %get-tuple-element.454, s32[]{:T(128)} %get-tuple-element.452, f32[256,10,128]{0,2,1:T(8,128)S(1)} %convolution_bitcast_fusion.3, f32[10,256]{1,0:T(8,128)S(1)} %bitcast.130, pred[256,256]{1,0:T(8,128)(4,1)S(1)} %fusion.47, ...), kind=kOutput, calls=%fused_computation.6.clone.1 | convolution fusion | flops 339148800 | bytes 4687872 | tf_op jit(solution)/shard_map/while/body/eval_jaxpr/nhcs,nshd->nchd/dot_general | solution.py:37
  242.5 3.2 %multiply_reduce_fusion = f32[4,256,10]{1,2,0:T(8,128)S(1)} fusion(f32[4,256,10,128]{1,3,2,0:T(8,128)} %get-tuple-element.137), kind=kLoop, calls=%fused_computation.38 | loop fusion | flops 2611200 | bytes 5283840 | tf_op jit(solution)/shard_map/reduce_sum | solution.py:113
  247.2 2.6 copy.99
  249.8 35.9 %all_to_all.80 = bf16[4,256,1280]{2,1,0:T(8,128)(2,1)S(1)} all-to-all(bf16[4,256,1280]{2,1,0:T(8,128)(2,1)} %copy.99), channel_id=1, replica_groups=mesh['seq'=32,'head'=4] {'head'}, dimensions={0} | all-to-all | bytes 5242880 | tf_op jit(solution)/shard_map/all_to_all | solution.py:137
  285.7 2.5 copy.100
  288.2 4.4 %copy.101 = bf16[256,5120]{1,0:T(8,128)(2,1)} copy(bf16[256,5120]{0,1:T(8,128)(2,1)} %bitcast.126) | data formatting | bytes 5242880 | tf_op jit(solution)/shard_map/all_to_all | solution.py:137
  (158 shorter events, 65.8 us)
Async XLA Ops:
  6.5 95.0 %copy-start = (f32[5120]{0:T(1024)S(1)}, f32[5120]{0:T(1024)}, u32[]{:S(2)}) copy-start(f32[5120]{0:T(1024)} %param.17) | copy-start | bytes 61444
  7.9 8.4 %all-to-all-start = ((bf16[256,4,10]{0,2,1:T(8,128)(2,1)}), bf16[256,4,10]{0,2,1:T(8,128)(2,1)S(1)}, u32[]{:S(2)}, u32[]{:S(2)}) async-start(bf16[256,4,10]{0,2,1:T(8,128)(2,1)} %all_to_all.60), calls=%async_computation | async-start | bytes 65536 | tf_op jit(solution)/shard_map/all_to_all | solution.py:123
  16.3 34.7 %all-to-all-start.1 = ((bf16[256,4,1280]{0,2,1:T(8,128)(2,1)}), bf16[256,4,1280]{0,2,1:T(8,128)(2,1)S(1)}, u32[]{:S(2)}, u32[]{:S(2)}) async-start(bf16[256,4,1280]{0,2,1:T(8,128)(2,1)} %bitcast.125), calls=%async_computation.1 | async-start | bytes 5242880 | tf_op jit(solution)/shard_map/all_to_all | solution.py:121
  51.0 1.5 copy-start.5
  52.5 34.2 %all-to-all-start.2 = ((bf16[256,4,1280]{0,2,1:T(8,128)(2,1)}), bf16[256,4,1280]{0,2,1:T(8,128)(2,1)}, u32[]{:S(2)}, u32[]{:S(2)}) async-start(bf16[256,4,1280]{0,2,1:T(8,128)(2,1)} %bitcast.123), calls=%async_computation.2 | async-start | bytes 5242880 | tf_op jit(solution)/shard_map/all_to_all | solution.py:122
  57.1 117.8 %all-gather.4.cloned.1.call-start = ((), (), s32[]{:S(2)}) async-start(), calls=%async_computation.5 | async-start | bytes 21626880 | tf_op jit(solution)/shard_map/all_gather | solution.py:11
  90.8 0.9 copy-start.3
  90.8 5.5 %copy-start.2 = (f32[4,10,128,128]{3,2,1,0:T(8,128)}, f32[4,10,128,128]{3,2,1,0:T(8,128)S(1)}, u32[]{:S(2)}) copy-start(f32[4,10,128,128]{3,2,1,0:T(8,128)S(1)} %get-tuple-element.477) | copy-start | bytes 7864324
  96.3 3.8 %copy-start.7 = (u32[128]{0:T(128)S(1)}, u32[128]{0:T(128)}, u32[]{:S(2)}) copy-start(u32[128]{0:T(128)} %constant.83) | copy-start | bytes 1540
  96.3 68.9 %all-to-all-start.3 = ((bf16[256,4,1280]{0,2,1:T(8,128)(2,1)}), bf16[256,4,1280]{0,2,1:T(8,128)(2,1)S(1)}, u32[]{:S(2)}, u32[]{:S(2)}) async-start(bf16[256,4,1280]{0,2,1:T(8,128)(2,1)} %bitcast.124), calls=%async_computation.3 | async-start | bytes 5242880 | tf_op jit(solution)/shard_map/all_to_all | solution.py:120
  165.2 2.3 copy-start.6
  242.5 4.0 %copy-start.4 = (f32[4,256,10,128]{1,3,2,0:T(8,128)S(1)}, f32[4,256,10,128]{1,3,2,0:T(8,128)}, u32[]{:S(2)}) copy-start(f32[4,256,10,128]{1,3,2,0:T(8,128)} %get-tuple-element.137) | copy-start | bytes 15728644
  288.2 4.4 %copy-start.1 = (f32[5120]{0:T(1024)S(1)}, f32[5120]{0:T(1024)}, u32[]{:S(2)}) copy-start(f32[5120]{0:T(1024)} %param.17) | copy-start | bytes 61444
Sparse Core Ops, SparseCore 0:
  91.8 82.9 all-gather.3
where the time goes:
time: 302 us; the launch traced here: 299 us
  blocking collectives  99.1 us (33%)
  waiting for transfers between devices  55.6 us (18%)
  other arithmetic  55.5 us (18%)
  local copies, waits for them, and re-layouts  32 us (11%)
  matrix products  24.7 us (8%)
  starting transfers between devices  16.6 us (5%)
  between operations  14.4 us (5%)
    unnamed x1, blocking collectives  63.2 us
    add x31, other arithmetic, combine_states(): later[0][:, None, None] * earlier[1] + later[1]  38.9 us
    all_to_all x1, blocking collectives, body(): lax.all_to_all(grouped, 'head', split_axis=0, concat_axis=1, tiled=True)  35.9 us
    all_to_all x1, waiting for transfers between devices, body(): lax.all_to_all(key_rows, 'head', split_axis=1, concat_axis=0, tiled=True)  26.1 us
    all_to_all x1, waiting for transfers between devices, body(): lax.all_to_all(value_rows, 'head', split_axis=1, concat_axis=0, tiled=True)  22.2 us
    unnamed x22, local copies, waits for them, and re-layouts  17.4 us
    dot_general x4, matrix products, block_local(): jnp.einsum('nhcs,nshd->nchd', weights, value_blocks, preferred_element_ty...  15.5 us
    all_to_all x3, local copies, waits for them, and re-layouts, body(): lax.all_to_all(grouped, 'head', split_axis=0, concat_axis=1, tiled=True)  9.5 us
  transfers between devices with their start and end apart: 5, of which 3 were waited for; matrix products, arithmetic and copies ran while one was open for 8% of the time, Pallas kernels for 0%

commit v1 on v0

--- a/solution.py
+++ b/solution.py
@@ -4,6 +4,29 @@
 from jax.sharding import PartitionSpec as P
 
 BLOCK = 256
+
+
+def in_blocks(shard, dim, size):
+    shape = shard.shape
+    tiles = shard.reshape(*shape[:dim], size, shape[dim] // size, *shape[dim + 1 :])
+    return jnp.moveaxis(tiles, dim, 0)
+
+
+def joined_along(parts, dim):
+    lengths = list(parts.shape[1:])
+    lengths[dim] *= parts.shape[0]
+    return jnp.moveaxis(parts, 0, dim).reshape(lengths)
+
+
+def pairwise_exchange(array, axis, split_dim, concat_dim):
+    devices, index = (lax.axis_size(axis), lax.axis_index(axis))
+    blocks = in_blocks(array, split_dim, devices)
+    done = [blocks[index]]
+    for lap in range(1, devices):
+        sent = blocks[index ^ lap]
+        done.append(lax.ppermute(sent, axis, [(i, i ^ lap) for i in range(devices)]))
+    blocks = jnp.stack(done)[index ^ jnp.arange(devices)]
+    return joined_along(blocks, concat_dim)
 
 
 def prefix(part, axis, combine, identity):
@@ -118,7 +141,7 @@
 def body(query_rows, key_rows, value_rows, log_decay, documents, norm_gain):
     query, keyed, valued, decays = (
         lax.all_to_all(query_rows, "head", split_axis=1, concat_axis=0, tiled=True),
-        lax.all_to_all(key_rows, "head", split_axis=1, concat_axis=0, tiled=True),
+        pairwise_exchange(key_rows, "head", 1, 0),
         lax.all_to_all(value_rows, "head", split_axis=1, concat_axis=0, tiled=True),
         lax.all_to_all(log_decay, "head", split_axis=1, concat_axis=0, tiled=True),
     )

time: 302 us -> 301 us (level)
  waiting for transfers between devices: 55.6 us -> 39.7 us
  local copies, waits for them, and re-layouts: 32 us -> 45.4 us
  other arithmetic: 55.5 us -> 58.9 us
    all_to_all x1 -> x0, waiting for transfers between devices: 26.1 us -> none  [body(): lax.all_to_all(key_rows, 'head', split_axis=1, concat_axis=0, tiled=True)]
    all_to_all x1, waiting for transfers between devices: 0.01 us -> 21.4 us  [body(): lax.all_to_all(log_decay, 'head', split_axis=1, concat_axis=0, tiled=True)]
    all_to_all x1, waiting for transfers between devices: 22.2 us -> 10.9 us  [body(): lax.all_to_all(value_rows, 'head', split_axis=1, concat_axis=0, tiled=True)]
    another operation x7 -> x12, local copies, waits for them, and re-layouts: 0.15 us -> 9.25 us
    gather x0 -> x2, local copies, waits for them, and re-layouts: none -> 8.33 us  [pairwise_exchange(): blocks = jnp.stack(done)[index ^ jnp.arange(devices)]]
    all_to_all x1 -> x0, starting transfers between devices: 4.24 us -> none  [body(): lax.all_to_all(key_rows, 'head', split_axis=1, concat_axis=0, tiled=True)]
    ppermute x0 -> x3, starting transfers between devices: none -> 3.86 us  [pairwise_exchange(): lax.ppermute(sent, axis, [(i, i ^ lap) for i in range(devices)])]
    another operation x4 -> x5, other arithmetic: 2.39 us -> 5.91 us  [the longest x1 3.52 us: pairwise_exchange(): blocks = jnp.stack(done)[index ^ jnp.arange(devices)]]
  transfers between devices with their start and end apart: 5 -> 7, of which waited for: 3 -> 3; matrix products, arithmetic and copies ran while one was open for 8% -> 12% of each run, Pallas kernels for 0% -> 0%
where the time goes in v1:
time: 301 us; the launch traced here: 299 us
  blocking collectives  99.1 us (33%)
  other arithmetic  58.9 us (20%)
  local copies, waits for them, and re-layouts  45.4 us (15%)
  waiting for transfers between devices  39.7 us (13%)
  matrix products  24.8 us (8%)
  starting transfers between devices  15.1 us (5%)
  between operations  14.2 us (5%)
    unnamed x1, blocking collectives  63.2 us
    add x31, other arithmetic, combine_states(): later[0][:, None, None] * earlier[1] + later[1]  38.9 us
    all_to_all x1, blocking collectives, body(): lax.all_to_all(grouped, 'head', split_axis=0, concat_axis=1, tiled=True)  35.9 us
    all_to_all x1, waiting for transfers between devices, body(): lax.all_to_all(log_decay, 'head', split_axis=1, concat_axis=0, tiled=True)  21.4 us
    dot_general x4, matrix products, block_local(): jnp.einsum('nhcs,nshd->nchd', weights, value_blocks, preferred_element_ty...  15.5 us
    unnamed x26, local copies, waits for them, and re-layouts  14.1 us
    all_to_all x1, waiting for transfers between devices, body(): lax.all_to_all(value_rows, 'head', split_axis=1, concat_axis=0, tiled=True)  10.9 us
    all_to_all x3, local copies, waits for them, and re-layouts, body(): lax.all_to_all(grouped, 'head', split_axis=0, concat_axis=1, tiled=True)  9.52 us
  transfers between devices with their start and end apart: 7, of which 3 were waited for; matrix products, arithmetic and copies ran while one was open for 12% of the time, Pallas kernels for 0%

profile of v1, /device:TPU:121, one launch (start us, length us, event | category | flops | bytes accessed | tf_op | source)
XLA Modules:
  0.0 298.6 jit_solution(4263559349699299405)
XLA Ops:
  6.5 3.0 copy.121
  21.0 3.7 %all-to-all-start = ((bf16[256,4,10]{0,2,1:T(8,128)(2,1)}), bf16[256,4,10]{0,2,1:T(8,128)(2,1)S(1)}, u32[]{:S(2)}, u32[]{:S(2)}) async-start(bf16[256,4,10]{0,2,1:T(8,128)(2,1)} %all_to_all.48), calls=%async_computation | async-start | bytes 65536 | tf_op jit(solution)/shard_map/all_to_all | solution.py:146
  29.7 21.4 %all-to-all-done = bf16[256,4,10]{0,2,1:T(8,128)(2,1)S(1)} async-done(((bf16[256,4,10]{0,2,1:T(8,128)(2,1)}), bf16[256,4,10]{0,2,1:T(8,128)(2,1)S(1)}, u32[]{:S(2)}, u32[]{:S(2)}) %all-to-all-start) | async-done | bytes 20512 | tf_op jit(solution)/shard_map/all_to_all | solution.py:146
  51.0 3.7 %all-to-all-start.1 = ((bf16[256,4,1280]{0,2,1:T(8,128)(2,1)}), bf16[256,4,1280]{0,2,1:T(8,128)(2,1)S(1)}, u32[]{:S(2)}, u32[]{:S(2)}) async-start(bf16[256,4,1280]{0,2,1:T(8,128)(2,1)} %bitcast.132), calls=%async_computation.1 | async-start | bytes 5242880 | tf_op jit(solution)/shard_map/all_to_all | solution.py:145
  61.8 3.5 %pad_maximum_fusion = bf16[4,256,1280]{2,1,0:T(8,128)(2,1)} fusion(bf16[1,256,1280]{2,1,0:T(8,128)(2,1)} %bitcast.29, bf16[1,256,1280]{2,1,0:T(8,128)(2,1)} %bitcast.27, bf16[1,256,1280]{2,1,0:T(8,128)(2,1)} %bitcast.25, bf16[1,256,1280]{2,1,0:T(8,128)(2,1)} %bitcast.136), kind=kLoop, calls=%fused_computation.43 | loop fusion | flops 3932160 | bytes 5242880 | tf_op jit(solution)/shard_map/stack | solution.py:28
  65.3 4.0 %gather_fusion = bf16[4,256,1280]{2,1,0:T(8,128)(2,1)} fusion(bf16[4,256,1280]{2,1,0:T(8,128)(2,1)} %pad_maximum_fusion, s32[1024]{0:T(1024)S(1)} %pad_clamp_fusion), kind=kCustom, calls=%fused_computation | custom fusion | bytes 5242896 | tf_op jit(solution)/shard_map/gather | solution.py:28
  69.3 4.4 %copy.126 = bf16[4,256,1280]{1,2,0:T(8,128)(2,1)} copy(bf16[4,256,1280]{2,1,0:T(8,128)(2,1)} %gather_fusion) | data formatting | bytes 5242880 | tf_op jit(solution)/shard_map/gather | solution.py:28
  73.6 10.9 %all-to-all-done.1 = bf16[256,4,1280]{0,2,1:T(8,128)(2,1)S(1)} async-done(((bf16[256,4,1280]{0,2,1:T(8,128)(2,1)}), bf16[256,4,1280]{0,2,1:T(8,128)(2,1)S(1)}, u32[]{:S(2)}, u32[]{:S(2)}) %all-to-all-start.1) | async-done | bytes 2621472 | tf_op jit(solution)/shard_map/all_to_all | solution.py:145
  86.1 3.4 %fusion.27 = f32[4,10,128,128]{3,2,1,0:T(8,128)S(1)} fusion(bf16[4,256,10,128]{1,3,2,0:T(8,128)(2,1)} %bitcast.126, bf16[4,256,10,128]{1,3,2,0:T(8,128)(2,1)} %bitcast.128, f32[4,256,10]{1,2,0:T(8,128)S(1)} %copy.128), kind=kOutput, calls=%fused_computation.42 | convolution fusion | flops 339476480 | bytes 7905280 | tf_op jit(solution)/shard_map/nchd,nche->nhde/dot_general | solution.py:84
  91.1 4.6 %copy.131 = bf16[256,5120]{0,1:T(8,128)(2,1)} copy(bf16[256,5120]{1,0:T(8,128)(2,1)} %param.12) | data formatting | bytes 5242880 | tf_op args[0]
  95.7 3.8 %all-to-all-start.2 = ((bf16[256,4,1280]{0,2,1:T(8,128)(2,1)}), bf16[256,4,1280]{0,2,1:T(8,128)(2,1)S(1)}, u32[]{:S(2)}, u32[]{:S(2)}) async-start(bf16[256,4,1280]{0,2,1:T(8,128)(2,1)} %bitcast.133), calls=%async_computation.2 | async-start | bytes 5242880 | tf_op jit(solution)/shard_map/all_to_all | solution.py:143
  101.0 63.2 %all-reduce = f32[320]{0:T(512)S(1)} all-reduce(f32[320]{0:T(512)S(1)} %dynamic-update-slice), channel_id=2, replica_groups=mesh['seq'=32,'head'=4] {'seq'}, use_global_device_ids=true, to_apply=%add | all-reduce | flops 320 | bytes 2560
  166.6 7.4 %all-gather.4.cloned.1.call-done = f32[320,128,128]{2,1,0:T(8,128)} async-done(((f32[10,128,128]{2,1,0:T(8,128)}), f32[320,128,128]{2,1,0:T(8,128)}) %all-gather.4.cloned.1.call-update) | async-done | bytes 20971536 | tf_op jit(solution)/shard_map/all_gather | solution.py:34
  174.1 40.4 %while.37 = (s32[]{:T(128)}, f32[10,128,128]{2,1,0:T(8,128)S(1)}, s32[]{:T(128)}, f32[32,10]{1,0:T(8,128)S(1)}, f32[32,10,128,128]{3,2,1,0:T(8,128)}, /*index=5*/s32[]{:T(128)}, s32[]{:T(128)}, s32[]{:T(128)}) while((s32[]{:T(128)}, f32[10,128,128]{2,1,0:T(8,128)S(1)}, s32[]{:T(128)}, f32[32,10]{1,0:T(8,128)S(1)}, ...), condition=%wide.region_5.6_spmd, body=%wide.region_4.5_spmd.sunk | while | flops 327685 | bytes 1966327 | solution.py:42
  214.5 27.1 %while.38 = (s32[]{:T(128)}, f32[10,128,128]{2,1,0:T(8,128)S(1)}, f32[4,256,10,128]{1,3,2,0:T(8,128)}, f32[4,10]{1,0:T(4,128)S(1)}, f32[4,10,128,128]{3,2,1,0:T(...) while((s32[]{:T(128)}, f32[10,128,128]{2,1,0:T(8,128)S(1)}, ...), condition=%wide.region_7.8_spmd, body=%wide.region_6.7_spmd.sunk | while | flops 423723008 | bytes 9385725 | solution.py:122
  216.2 3.9 %fusion.49 = f32[4,256,10,128]{1,3,2,0:T(8,128)} fusion(f32[4,256,10,128]{1,3,2,0:T(8,128)} %get-tuple-element.469, s32[]{:T(128)} %get-tuple-element.467, f32[256,10,128]{0,2,1:T(8,128)S(1)} %convolution_bitcast_fusion.3, f32[10,256]{1,0:T(8,128)S(1)} %bitcast.143, pred[256,256]{1,0:T(8,128)(4,1)S(1)} %fusion.48, ...), kind=kOutput, calls=%fused_computation.7.clone.1 | convolution fusion | flops 339148800 | bytes 4687872 | tf_op jit(solution)/shard_map/while/body/eval_jaxpr/nhcs,nshd->nchd/dot_general | solution.py:60
  222.9 3.9 %fusion.49 = f32[4,256,10,128]{1,3,2,0:T(8,128)} fusion(f32[4,256,10,128]{1,3,2,0:T(8,128)} %get-tuple-element.469, s32[]{:T(128)} %get-tuple-element.467, f32[256,10,128]{0,2,1:T(8,128)S(1)} %convolution_bitcast_fusion.3, f32[10,256]{1,0:T(8,128)S(1)} %bitcast.143, pred[256,256]{1,0:T(8,128)(4,1)S(1)} %fusion.48, ...), kind=kOutput, calls=%fused_computation.7.clone.1 | convolution fusion | flops 339148800 | bytes 4687872 | tf_op jit(solution)/shard_map/while/body/eval_jaxpr/nhcs,nshd->nchd/dot_general | solution.py:60
  229.7 3.8 %fusion.49 = f32[4,256,10,128]{1,3,2,0:T(8,128)} fusion(f32[4,256,10,128]{1,3,2,0:T(8,128)} %get-tuple-element.469, s32[]{:T(128)} %get-tuple-element.467, f32[256,10,128]{0,2,1:T(8,128)S(1)} %convolution_bitcast_fusion.3, f32[10,256]{1,0:T(8,128)S(1)} %bitcast.143, pred[256,256]{1,0:T(8,128)(4,1)S(1)} %fusion.48, ...), kind=kOutput, calls=%fused_computation.7.clone.1 | convolution fusion | flops 339148800 | bytes 4687872 | tf_op jit(solution)/shard_map/while/body/eval_jaxpr/nhcs,nshd->nchd/dot_general | solution.py:60
  236.5 3.9 %fusion.49 = f32[4,256,10,128]{1,3,2,0:T(8,128)} fusion(f32[4,256,10,128]{1,3,2,0:T(8,128)} %get-tuple-element.469, s32[]{:T(128)} %get-tuple-element.467, f32[256,10,128]{0,2,1:T(8,128)S(1)} %convolution_bitcast_fusion.3, f32[10,256]{1,0:T(8,128)S(1)} %bitcast.143, pred[256,256]{1,0:T(8,128)(4,1)S(1)} %fusion.48, ...), kind=kOutput, calls=%fused_computation.7.clone.1 | convolution fusion | flops 339148800 | bytes 4687872 | tf_op jit(solution)/shard_map/while/body/eval_jaxpr/nhcs,nshd->nchd/dot_general | solution.py:60
  241.7 3.2 %multiply_reduce_fusion = f32[4,256,10]{1,2,0:T(8,128)S(1)} fusion(f32[4,256,10,128]{1,3,2,0:T(8,128)} %get-tuple-element.137), kind=kLoop, calls=%fused_computation.39 | loop fusion | flops 2611200 | bytes 5283840 | tf_op jit(solution)/shard_map/reduce_sum | solution.py:136
  246.4 2.6 copy.137
  249.0 35.9 %all_to_all.64 = bf16[4,256,1280]{2,1,0:T(8,128)(2,1)S(1)} all-to-all(bf16[4,256,1280]{2,1,0:T(8,128)(2,1)} %copy.137), channel_id=1, replica_groups=mesh['seq'=32,'head'=4] {'head'}, dimensions={0} | all-to-all | bytes 5242880 | tf_op jit(solution)/shard_map/all_to_all | solution.py:160
  284.8 2.6 copy.138
  287.4 4.4 %copy.139 = bf16[256,5120]{1,0:T(8,128)(2,1)} copy(bf16[256,5120]{0,1:T(8,128)(2,1)} %bitcast.135) | data formatting | bytes 5242880 | tf_op jit(solution)/shard_map/all_to_all | solution.py:160
  (176 shorter events, 82.6 us)
Async XLA Ops:
  6.5 94.1 %copy-start = (f32[5120]{0:T(1024)S(1)}, f32[5120]{0:T(1024)}, u32[]{:S(2)}) copy-start(f32[5120]{0:T(1024)} %param.17) | copy-start | bytes 61444
  10.9 9.5 %copy-start.8 = (bf16[256,40]{0,1:T(8,128)(2,1)S(1)}, bf16[256,40]{0,1:T(8,128)(2,1)}, u32[]{:S(2)}) copy-start(bf16[256,40]{0,1:T(8,128)(2,1)} %param.15) | copy-start | bytes 61444
  10.9 16.2 %copy-start.7 = (bf16[256,5120]{1,0:T(8,128)(2,1)S(1)}, bf16[256,5120]{1,0:T(8,128)(2,1)}, u32[]{:S(2)}) copy-start(bf16[256,5120]{1,0:T(8,128)(2,1)} %param.14) | copy-start | bytes 7864324
  13.2 48.6 %collective-permute-start = (bf16[256,1280]{1,0:T(8,128)(2,1)}, bf16[256,1280]{1,0:T(8,128)(2,1)}, u32[]{:S(2)}, u32[]{:S(2)}) collective-permute-start(bf16[256,1280]{1,0:T(8,128)(2,1)} %bitcast.137), channel_id=1, source_target_pairs={{0,1},{1,0},{2,3},{3,2},{4,5},{5,4},{6,7},{7,6},{8,9},{9,8},{10,11... | collective-permute-start | bytes 1966088 | tf_op jit(solution)/shard_map/ppermute | solution.py:27
  16.6 45.2 %collective-permute-start.1 = (bf16[256,1280]{1,0:T(8,128)(2,1)}, bf16[256,1280]{1,0:T(8,128)(2,1)}, u32[]{:S(2)}, u32[]{:S(2)}) collective-permute-start(bf16[256,1280]{1,0:T(8,128)(2,1)} %bitcast.138), channel_id=1, source_target_pairs={{0,2},{1,3},{2,0},{3,1},{4,6},{5,7},{6,4},{7,5},{8,10},{9,11},{10,... | collective-permute-start | bytes 1966088 | tf_op jit(solution)/shard_map/ppermute | solution.py:27
  20.1 41.6 %collective-permute-start.2 = (bf16[256,1280]{1,0:T(8,128)(2,1)}, bf16[256,1280]{1,0:T(8,128)(2,1)}, u32[]{:S(2)}, u32[]{:S(2)}) collective-permute-start(bf16[256,1280]{1,0:T(8,128)(2,1)} %bitcast.139), channel_id=1, source_target_pairs={{0,3},{1,2},{2,1},{3,0},{4,7},{5,6},{6,5},{7,4},{8,11},{9,10},{10,... | collective-permute-start | bytes 1966088 | tf_op jit(solution)/shard_map/ppermute | solution.py:27
  21.0 30.1 %all-to-all-start = ((bf16[256,4,10]{0,2,1:T(8,128)(2,1)}), bf16[256,4,10]{0,2,1:T(8,128)(2,1)S(1)}, u32[]{:S(2)}, u32[]{:S(2)}) async-start(bf16[256,4,10]{0,2,1:T(8,128)(2,1)} %all_to_all.48), calls=%async_computation | async-start | bytes 65536 | tf_op jit(solution)/shard_map/all_to_all | solution.py:146
  51.0 33.5 %all-to-all-start.1 = ((bf16[256,4,1280]{0,2,1:T(8,128)(2,1)}), bf16[256,4,1280]{0,2,1:T(8,128)(2,1)S(1)}, u32[]{:S(2)}, u32[]{:S(2)}) async-start(bf16[256,4,1280]{0,2,1:T(8,128)(2,1)} %bitcast.132), calls=%async_computation.1 | async-start | bytes 5242880 | tf_op jit(solution)/shard_map/all_to_all | solution.py:145
  54.7 119.3 %all-gather.4.cloned.1.call-start = ((), (), s32[]{:S(2)}) async-start(), calls=%async_computation.4 | async-start | bytes 21626880 | tf_op jit(solution)/shard_map/all_gather | solution.py:34
  84.6 1.5 copy-start.5
  90.2 0.9 copy-start.3
  90.2 5.5 %copy-start.2 = (f32[4,10,128,128]{3,2,1,0:T(8,128)}, f32[4,10,128,128]{3,2,1,0:T(8,128)S(1)}, u32[]{:S(2)}) copy-start(f32[4,10,128,128]{3,2,1,0:T(8,128)S(1)} %get-tuple-element.492) | copy-start | bytes 7864324
  95.7 3.8 %copy-start.9 = (u32[128]{0:T(128)S(1)}, u32[128]{0:T(128)}, u32[]{:S(2)}) copy-start(u32[128]{0:T(128)} %constant.92) | copy-start | bytes 1540
  95.7 68.6 %all-to-all-start.2 = ((bf16[256,4,1280]{0,2,1:T(8,128)(2,1)}), bf16[256,4,1280]{0,2,1:T(8,128)(2,1)S(1)}, u32[]{:S(2)}, u32[]{:S(2)}) async-start(bf16[256,4,1280]{0,2,1:T(8,128)(2,1)} %bitcast.133), calls=%async_computation.2 | async-start | bytes 5242880 | tf_op jit(solution)/shard_map/all_to_all | solution.py:143
  164.4 2.3 copy-start.6
  241.7 4.0 %copy-start.4 = (f32[4,256,10,128]{1,3,2,0:T(8,128)S(1)}, f32[4,256,10,128]{1,3,2,0:T(8,128)}, u32[]{:S(2)}) copy-start(f32[4,256,10,128]{1,3,2,0:T(8,128)} %get-tuple-element.137) | copy-start | bytes 15728644
  287.4 4.4 %copy-start.1 = (f32[5120]{0:T(1024)S(1)}, f32[5120]{0:T(1024)}, u32[]{:S(2)}) copy-start(f32[5120]{0:T(1024)} %param.17) | copy-start | bytes 61444
Sparse Core Ops, SparseCore 0:
  91.2 82.7 all-gather.3
